TPU v7x, 32 devices: a whole 2x2x4 slice. The times are simulated.
32 devices in a mesh: groups: 2 (over y), ep: 4 (over z), tp: 2 (over x), sp: 2 (over core).
Axes of the slice: x: 2, y: 2, z: 4, core: 2. Of those that a mesh axis runs over, the one named last changes fastest.
Arguments:
- logits: float32 [2048, 128], P(('groups', 'ep', 'sp')), parts along dimension 0, may hold values from -30 to 410
- routes: int32 [2048, 8], P(('groups', 'ep', 'sp')), parts along dimension 0, may hold values from 0 to 127, as said below
- owner: int32 [2048], P(('groups', 'ep', 'sp')), parts along dimension 0, may hold values from 0 to 1023, as said below
- tokens: bfloat16 [2048, 4096], P(('groups', 'ep', 'sp')), parts along dimension 0, may hold values from -6 to 6
- out_grad: bfloat16 [2048, 4096], P(('groups', 'ep', 'sp')), parts along dimension 0, may hold values from -6 to 6
- resp_lengths: int32 [16], P(('groups', 'ep', 'sp')), parts along dimension 0, may hold values from 1 to 128
- w_gate: bfloat16 [4, 4096, 1536], P('ep', None, 'tp'), may hold values from -0.09375 to 0.09375
- w_up: bfloat16 [4, 4096, 1536], P('ep', None, 'tp'), may hold values from -0.09375 to 0.09375
- w_down: bfloat16 [4, 1536, 4096], P('ep', 'tp'), may hold values from -0.15625 to 0.15625
Outputs:
- layer_out: bfloat16 [2048, 4096], P(('groups', 'ep', 'sp'), 'tp'), parts along dimension 0
- token_grad: bfloat16 [2048, 4096], P(('groups', 'ep', 'sp'), 'tp'), parts along dimension 0
- router_grad: float32 [2048, 128], P(('groups', 'ep', 'sp')), parts along dimension 0
There are 2 independent parts, one for each index of `groups`. A program takes and returns all parts, laid end to end along the dimension named above; an argument that names none is the same for every part. Nothing has to cross between parts.
Inputs may be any that keep to these rules, and one draw needn't show every extreme that they name: owner is a permutation of the group's 1024 token positions. Of the 128 rows of one device (aligned blocks in rollout order) at most 32 go to the 128 tokens of one owner (aligned blocks in learner order), and some such pair reaches 32. `routes`: each row names 8 different experts, exactly one of them below 4. Among the 128 tokens of any one owner (the rows that `owner` maps into that owner's block), no expert below 4 is named by more than 64 of them, and for every owner some expert below 4 is named by exactly 64.
All inputs are finite; a program needn't handle non-finite values.
Results may differ from a plain program's by a relative error of at most 0.0095.
Values may be sent and summed in bfloat16 or wider, within the bound.
A program may use at most 128 MiB of HBM per device.

v0:
```python
import jax
import jax.numpy as jnp
from jax import lax
from jax.sharding import PartitionSpec as P


def softmax_rows(values):
    highest = jnp.max(values, axis=1, keepdims=True)
    raised = jnp.exp(values - highest)
    return raised / jnp.sum(raised, axis=1, keepdims=True)


def slot_ranks(labels, total_labels):
    matches = (labels[:, None] == jnp.arange(total_labels, dtype=jnp.int32)[None, :]).astype(
        jnp.int32
    )
    return jnp.sum((jnp.cumsum(matches, axis=0) - 1) * matches, axis=1)


def place_rows(values, target, slot_count, filler):
    buffer = jnp.full((slot_count,) + values.shape[1:], filler, values.dtype)
    return buffer.at[target].set(values)


def to_experts(values, local_count):
    senders = values.shape[0]
    shaped = values.reshape(
        (senders, local_count, values.shape[1] // local_count) + values.shape[2:]
    )
    shaped = jnp.swapaxes(shaped, 0, 1)
    return shaped.reshape((local_count, senders * shaped.shape[2]) + values.shape[2:])


def from_experts(values, senders):
    local_count = values.shape[0]
    shaped = values.reshape((local_count, senders, values.shape[1] // senders) + values.shape[2:])
    shaped = jnp.swapaxes(shaped, 0, 1)
    return shaped.reshape((senders, local_count * shaped.shape[2]) + values.shape[2:])


def shards(logits, routes, owner, tokens, out_grad, resp_lengths, w_gate, w_up, w_down):
    tok_count = tokens.shape[0]
    ep_count = lax.axis_size("ep")
    tp_count = lax.axis_size("tp")
    owner_count = ep_count * lax.axis_size("sp")
    local_count = w_gate.shape[0]
    expert_count = local_count * ep_count
    per_owner = 2 * tok_count // owner_count
    per_expert = 2 * tok_count // expert_count
    owner_slots = owner_count * per_owner
    destination = owner // tok_count
    arrival = owner % tok_count
    target = destination * per_owner + slot_ranks(destination, owner_count)

    def send_rows(values, filler):
        placed = place_rows(values, target, owner_slots, filler)
        return placed.reshape((owner_count, per_owner) + values.shape[1:])

    route_values = routes.astype(jnp.float32)
    arrival_values = arrival.astype(jnp.float32)
    rows_in, routes_in, arrival_in = (
        lax.all_to_all(
            send_rows(logits, 0.0), ("ep", "sp"), split_axis=0, concat_axis=0, tiled=True
        ),
        lax.all_to_all(
            send_rows(route_values, 0.0), ("ep", "sp"), split_axis=0, concat_axis=0, tiled=True
        ),
        lax.all_to_all(
            send_rows(arrival_values, -1.0), ("ep", "sp"), split_axis=0, concat_axis=0, tiled=True
        ),
    )
    landing = jnp.where(arrival_in < 0, tok_count, arrival_in).astype(jnp.int32).reshape(-1)
    learner_logits = place_rows(
        rows_in.reshape(owner_slots, logits.shape[1]), landing, tok_count + 1, 0.0
    )[:tok_count]
    learner_routes = place_rows(
        routes_in.reshape(owner_slots, routes.shape[1]), landing, tok_count + 1, 0.0
    )[:tok_count].astype(jnp.int32)
    picked = jnp.take_along_axis(learner_logits, learner_routes, axis=1)
    gate_weights = softmax_rows(picked)
    in_window = learner_routes < expert_count
    expert_ids = jnp.sum(jnp.where(in_window, learner_routes, 0), axis=1)
    weight = jnp.sum(jnp.where(in_window, gate_weights, 0.0), axis=1)
    weight_b = weight.astype(jnp.bfloat16)
    live_mask = jnp.arange(tok_count, dtype=jnp.int32) < resp_lengths[0]
    masked_grad = jnp.where(live_mask[:, None], out_grad, jnp.zeros_like(out_grad))
    expert_slots = expert_count * per_expert
    slot_index = expert_ids * per_expert + slot_ranks(expert_ids, expert_count)

    def pack(values):
        placed = place_rows(values, slot_index, expert_slots, 0)
        return placed.reshape((ep_count, local_count * per_expert) + values.shape[1:])

    tokens_in, grads_in, scale_in = (
        lax.all_to_all(pack(tokens), "ep", split_axis=0, concat_axis=0, tiled=True),
        lax.all_to_all(pack(masked_grad), "ep", split_axis=0, concat_axis=0, tiled=True),
        lax.all_to_all(pack(weight_b), "ep", split_axis=0, concat_axis=0, tiled=True),
    )
    token_rows = to_experts(tokens_in, local_count)
    grad_rows = to_experts(grads_in, local_count)
    pre_gate = jnp.einsum("emd,edf->emf", token_rows, w_gate, preferred_element_type=jnp.float32)
    pre_up = jnp.einsum("emd,edf->emf", token_rows, w_up, preferred_element_type=jnp.float32)
    down_back = jnp.einsum("emd,efd->emf", grad_rows, w_down, preferred_element_type=jnp.float32)
    gate_scale = to_experts(scale_in, local_count).astype(jnp.float32)
    gate_sigmoid = jax.nn.sigmoid(pre_gate)
    active = pre_gate * gate_sigmoid
    hidden = (active * pre_up).astype(jnp.bfloat16)
    out_terms = (
        jnp.einsum("emf,efd->emd", hidden, w_down, preferred_element_type=jnp.float32)
        * gate_scale[:, :, None]
    )
    score_terms = jnp.sum(hidden.astype(jnp.float32) * down_back, axis=2)
    grad_hidden = gate_scale[:, :, None] * down_back
    grad_up = (grad_hidden * active).astype(jnp.bfloat16)
    grad_gate = (
        grad_hidden * pre_up * (gate_sigmoid * (1.0 + pre_gate * (1.0 - gate_sigmoid)))
    ).astype(jnp.bfloat16)
    grad_terms = jnp.einsum("emf,edf->emd", grad_gate, w_gate, preferred_element_type=jnp.float32)
    grad_terms = grad_terms + jnp.einsum(
        "emf,edf->emd", grad_up, w_up, preferred_element_type=jnp.float32
    )
    score_columns = jnp.broadcast_to(score_terms[:, :, None], score_terms.shape + (tp_count,))
    out_share, grad_share, score_share = (
        lax.psum_scatter(
            out_terms.astype(jnp.bfloat16), "tp", scatter_dimension=2, tiled=True
        ).astype(jnp.float32),
        lax.psum_scatter(
            grad_terms.astype(jnp.bfloat16), "tp", scatter_dimension=2, tiled=True
        ).astype(jnp.float32),
        lax.psum_scatter(
            score_columns.astype(jnp.bfloat16), "tp", scatter_dimension=2, tiled=True
        ).astype(jnp.float32),
    )
    out_back = from_experts(out_share.astype(jnp.bfloat16), ep_count)
    grad_back = from_experts(grad_share.astype(jnp.bfloat16), ep_count)
    score_back = from_experts(score_share[:, :, 0].astype(jnp.bfloat16), ep_count)
    out_home, grad_home, score_home = (
        lax.all_to_all(out_back, "ep", split_axis=0, concat_axis=0, tiled=True),
        lax.all_to_all(grad_back, "ep", split_axis=0, concat_axis=0, tiled=True),
        lax.all_to_all(score_back, "ep", split_axis=0, concat_axis=0, tiled=True),
    )
    share_width = out_home.shape[2]
    layer_out = out_home.reshape(expert_slots, share_width)[slot_index]
    token_grad = grad_home.reshape(expert_slots, share_width)[slot_index]
    token_score = score_home.reshape(expert_slots)[slot_index].astype(jnp.float32)
    route_grad = (
        token_score[:, None] * weight[:, None] * (in_window.astype(jnp.float32) - gate_weights)
    )
    columns = jnp.arange(logits.shape[1], dtype=jnp.int32)
    router_grad = jnp.sum(
        jnp.where(
            learner_routes[:, :, None] == columns[None, None, :], route_grad[:, :, None], 0.0
        ),
        axis=1,
    )
    return (layer_out, token_grad, router_grad)


def solution(mesh):
    in_specs = (
        P(("groups", "ep", "sp"), None),
        P(("groups", "ep", "sp"), None),
        P(("groups", "ep", "sp")),
        P(("groups", "ep", "sp"), None),
        P(("groups", "ep", "sp"), None),
        P(("groups", "ep", "sp")),
        P("ep", None, "tp"),
        P("ep", None, "tp"),
        P("ep", "tp", None),
    )
    out_specs = (
        P(("groups", "ep", "sp"), "tp"),
        P(("groups", "ep", "sp"), "tp"),
        P(("groups", "ep", "sp"), None),
    )
    return jax.shard_map(shards, mesh=mesh, in_specs=in_specs, out_specs=out_specs, check_vma=False)
```

profile of v0, /device:TPU:0, one launch (start us, length us, event | category | flops | bytes accessed | tf_op | source)
XLA Modules:
  0.0 302.7 jit_solution(14801856415097197084)
XLA Ops:
  9.9 6.3 %all-to-all-start = ((f32[8,1,32]{2,1,0:T(1,128)}), f32[8,1,32]{2,1,0:T(1,128)S(1)}, u32[]{:S(2)}, u32[]{:S(2)}) async-start(f32[8,1,32]{2,1,0:T(1,128)} %all_to_all.36), calls=%async_computation | async-start | bytes 8192 | tf_op jit(solution)/shard_map/all_to_all | solution.py:68
  30.6 3.4 %all-to-all-start.3 = ((f32[8,32,128]{2,1,0:T(8,128)}), f32[8,32,128]{2,1,0:T(8,128)S(1)}, u32[]{:S(2)}, u32[]{:S(2)}) async-start(f32[8,32,128]{2,1,0:T(8,128)} %bitcast.10), calls=%async_computation.3 | async-start | bytes 262144 | tf_op jit(solution)/shard_map/all_to_all | solution.py:62
  36.7 4.1 %all-to-all-done.3 = f32[8,32,128]{2,1,0:T(8,128)S(1)} async-done(((f32[8,32,128]{2,1,0:T(8,128)}), f32[8,32,128]{2,1,0:T(8,128)S(1)}, u32[]{:S(2)}, u32[]{:S(2)}) %all-to-all-start.3) | async-done | bytes 131104 | tf_op jit(solution)/shard_map/all_to_all | solution.py:62
  41.9 6.8 %gather_fusion.3 = f32[1024]{0:T(1024)S(1)} fusion(f32[128,128]{1,0:T(8,128)S(1)} %slice.17, s32[1024]{0:T(1024)S(1)} %reshape.265), kind=kCustom, calls=%fused_computation.3 | custom fusion | bytes 16384 | tf_op jit(solution)/shard_map/jit(take_along_axis)/gather | solution.py:79
  49.9 4.4 %scatter_custom_fusion.3 = bf16[256,4096]{1,0:T(8,128)(2,1)} fusion(s32[128]{0:T(128)S(1)} %fusion.56, bf16[128,4096]{1,0:T(8,128)(2,1)} %param.12, bf16[]{:T(256)} %constant.37.clone.1), kind=kCustom, calls=%fused_computation.33 | custom fusion | bytes 2097664 | tf_op jit(solution)/shard_map/scatter | solution.py:22
  54.2 3.6 %all-to-all-start.2 = ((bf16[4,64,4096]{2,1,0:T(8,128)(2,1)}), bf16[4,64,4096]{2,1,0:T(8,128)(2,1)S(1)}, u32[]{:S(2)}, u32[]{:S(2)}) async-start(bf16[4,64,4096]{2,1,0:T(8,128)(2,1)} %bitcast.5), calls=%async_computation.2 | async-start | bytes 4194304 | tf_op jit(solution)/shard_map/all_to_all | solution.py:95
  58.5 3.7 %scatter_custom_fusion.7 = bf16[256,4096]{1,0:T(8,128)(2,1)} fusion(s32[128]{0:T(128)S(1)} %fusion.56, bf16[128,4096]{1,0:T(8,128)(2,1)S(1)} %copy-done, bf16[]{:T(256)} %constant.37.clone.1, pred[128]{0:T(512)(128)(4,1)S(1)} %iota_compare_fusion.3), kind=kCustom, calls=%fused_computation.30 | custom fusion | flops 524288 | bytes 3147264 | tf_op jit(solution)/shard_map/scatter | solution.py:22
  62.2 43.8 %all-to-all-done.2 = bf16[4,64,4096]{2,1,0:T(8,128)(2,1)S(1)} async-done(((bf16[4,64,4096]{2,1,0:T(8,128)(2,1)}), bf16[4,64,4096]{2,1,0:T(8,128)(2,1)S(1)}, u32[]{:S(2)}, u32[]{:S(2)}) %all-to-all-start.2) | async-done | bytes 2097184 | tf_op jit(solution)/shard_map/all_to_all | solution.py:95
  106.0 4.6 %all-to-all-start.6 = ((bf16[4,64,4096]{2,1,0:T(8,128)(2,1)}), bf16[4,64,4096]{2,1,0:T(8,128)(2,1)}, u32[]{:S(2)}, u32[]{:S(2)}) async-start(bf16[4,64,4096]{2,1,0:T(8,128)(2,1)} %bitcast.17), calls=%async_computation.7 | async-start | bytes 4194304 | tf_op jit(solution)/shard_map/all_to_all | solution.py:96
  111.2 5.5 %fusion.10 = f32[256,768]{1,0:T(8,128)} fusion(bf16[256,4096]{1,0:T(8,128)(2,1)S(1)} %bitcast.71, bf16[1,4096,768]{2,1,0:T(8,128)(2,1)} %param.15), kind=kOutput, calls=%fused_computation.22 | convolution fusion | flops 1610612736 | bytes 9175040 | tf_op jit(solution)/shard_map/emd,edf->emf/dot_general | solution.py:101
  116.7 5.4 %fusion.6 = f32[256,768]{1,0:T(8,128)} fusion(bf16[256,4096]{1,0:T(8,128)(2,1)S(1)} %bitcast.72, bf16[1,4096,768]{2,1,0:T(8,128)(2,1)} %param.16), kind=kOutput, calls=%fused_computation.18 | convolution fusion | flops 1610612736 | bytes 9175040 | tf_op jit(solution)/shard_map/emd,edf->emf/dot_general | solution.py:102
  122.1 36.1 %all-to-all-done.6 = bf16[4,64,4096]{2,1,0:T(8,128)(2,1)} async-done(((bf16[4,64,4096]{2,1,0:T(8,128)(2,1)}), bf16[4,64,4096]{2,1,0:T(8,128)(2,1)}, u32[]{:S(2)}, u32[]{:S(2)}) %all-to-all-start.6) | async-done | bytes 2097184 | tf_op jit(solution)/shard_map/all_to_all | solution.py:96
  158.2 6.8 %multiply_reduce_fusion = (bf16[256]{0:T(256)(128)(2,1)S(1)}, bf16[256,768]{1,0:T(8,128)(2,1)}, f32[256,768]{1,0:T(8,128)}) fusion(f32[256,768]{1,0:T(8,128)} %fusion.6, f32[256,768]{1,0:T(8,128)} %fusion.10, bf16[256,4096]{1,0:T(8,128)(2,1)} %bitcast.18, bf16[1,768,4096]{2,1,0:T(8,128)(2,1)} %param.17), kind=kOutput, calls=%fused_computation.36 | convolution fusion | flops 1612381952 | bytes 11141632 | tf_op jit(solution)/shard_map/emd,efd->emf/dot_general | solution.py:103
  164.9 4.9 %all-reduce = bf16[1,256,2]{1,2,0:T(2,128)(2,1)S(1)} all-reduce(bf16[1,256,2]{1,2,0:T(2,128)(2,1)S(1)} %broadcast_in_dim.100), channel_id=4, replica_groups=mesh['groups'=2,'ep'=4,'tp'=2,'sp'=2] {'tp'}, use_global_device_ids=true, to_apply=%region_19.20.clone | all-reduce | flops 512 | bytes 2048
  174.5 5.4 %all-to-all-done.8 = bf16[4,1,64]{2,1,0:T(2,128)(2,1)S(1)} async-done(((bf16[4,1,64]{2,1,0:T(2,128)(2,1)}), bf16[4,1,64]{2,1,0:T(2,128)(2,1)S(1)}, u32[]{:S(2)}, u32[]{:S(2)}) %all-to-all-start.8) | async-done | bytes 544 | tf_op jit(solution)/shard_map/all_to_all | solution.py:140
  182.7 7.9 %all_to_all.58 = bf16[4,1,64]{2,1,0:T(2,128)(2,1)S(1)} all-to-all(bf16[4,1,64]{2,1,0:T(2,128)(2,1)S(1)} %all_to_all.48), channel_id=1, replica_groups=mesh['groups'=2,'ep'=4,'tp'=2,'sp'=2] {'ep'}, dimensions={0} | all-to-all | bytes 1024 | tf_op jit(solution)/shard_map/all_to_all | solution.py:97
  190.7 5.2 %fusion.4 = f32[256,4096]{1,0:T(8,128)S(1)} fusion(bf16[1,4096,768]{2,1,0:T(8,128)(2,1)} %param.16, f32[256,768]{1,0:T(8,128)} %get-tuple-element.14, f32[256]{0:T(256)S(1)} %reshape.240, f32[256,768]{1,0:T(8,128)S(1)} %copy-done.1), kind=kOutput, calls=%fused_computation.16 | convolution fusion | flops 1611988992 | bytes 12059648 | tf_op jit(solution)/shard_map/emf,edf->emd/dot_general | solution.py:119
  195.9 3.5 %fusion.27 = bf16[1,256,4096]{2,1,0:T(8,128)(2,1)} fusion(f32[256,4096]{1,0:T(8,128)S(1)} %fusion.4, bf16[1,4096,768]{2,1,0:T(8,128)(2,1)S(1)} %bitcast.70, f32[256,768]{1,0:T(8,128)S(1)} %copy-done.1, f32[256,768]{1,0:T(8,128)S(1)} %copy-done.2, f32[256,768]{1,0:T(8,128)S(1)} %copy-done.3, f32[256]{0:T(256)S(1)} %reshape.240), kind=kOutput, calls=%fused_computation.29 | convolution fusion | flops 1614872576 | bytes 14943232 | tf_op jit(solution)/shard_map/emf,edf->emd/dot_general | solution.py:118
  199.4 6.0 %fusion.24 = bf16[1,256,4096]{2,1,0:T(8,128)(2,1)} fusion(bf16[256,768]{1,0:T(8,128)(2,1)} %get-tuple-element.4, bf16[1,768,4096]{2,1,0:T(8,128)(2,1)} %param.17, f32[256]{0:T(256)S(1)} %reshape.240), kind=kOutput, calls=%fused_computation.28 | convolution fusion | flops 1612709888 | bytes 8782848 | tf_op jit(solution)/shard_map/emf,efd->emd/dot_general | solution.py:109
  205.5 24.1 %reduce-scatter.6.cloned.1.call-done = bf16[1,256,2048]{2,1,0:T(8,128)(2,1)} async-done(((bf16[1,256,4096]{2,1,0:T(8,128)(2,1)}), bf16[1,256,2048]{2,1,0:T(8,128)(2,1)}) %reduce-scatter.6.cloned.1.call-update) | async-done | bytes 1048592 | tf_op jit(solution)/shard_map/reduce_scatter | solution.py:127
  229.6 4.6 %all-to-all-start.7 = ((bf16[4,64,2048]{2,1,0:T(8,128)(2,1)}), bf16[4,64,2048]{2,1,0:T(8,128)(2,1)S(1)}, u32[]{:S(2)}, u32[]{:S(2)}) async-start(bf16[4,64,2048]{2,1,0:T(8,128)(2,1)} %bitcast.74), calls=%async_computation.9 | async-start | bytes 2097152 | tf_op jit(solution)/shard_map/all_to_all | solution.py:139
  234.2 29.6 %reduce-scatter.4.cloned.1.call-done = bf16[1,256,2048]{2,1,0:T(8,128)(2,1)} async-done(((bf16[1,256,4096]{2,1,0:T(8,128)(2,1)}), bf16[1,256,2048]{2,1,0:T(8,128)(2,1)}) %reduce-scatter.4.cloned.1.call-update) | async-done | bytes 1048592 | tf_op jit(solution)/shard_map/reduce_scatter | solution.py:124
  263.8 4.6 %all-to-all-start.5 = ((bf16[4,64,2048]{2,1,0:T(8,128)(2,1)}), bf16[4,64,2048]{2,1,0:T(8,128)(2,1)S(1)}, u32[]{:S(2)}, u32[]{:S(2)}) async-start(bf16[4,64,2048]{2,1,0:T(8,128)(2,1)} %bitcast.73), calls=%async_computation.6 | async-start | bytes 2097152 | tf_op jit(solution)/shard_map/all_to_all | solution.py:138
  271.2 22.9 %all-to-all-done.5 = bf16[4,64,2048]{2,1,0:T(8,128)(2,1)S(1)} async-done(((bf16[4,64,2048]{2,1,0:T(8,128)(2,1)}), bf16[4,64,2048]{2,1,0:T(8,128)(2,1)S(1)}, u32[]{:S(2)}, u32[]{:S(2)}) %all-to-all-start.5) | async-done | bytes 1048608 | tf_op jit(solution)/shard_map/all_to_all | solution.py:138
  (77 shorter events, 34.7 us)
Async XLA Ops:
  9.9 11.8 %all-to-all-start = ((f32[8,1,32]{2,1,0:T(1,128)}), f32[8,1,32]{2,1,0:T(1,128)S(1)}, u32[]{:S(2)}, u32[]{:S(2)}) async-start(f32[8,1,32]{2,1,0:T(1,128)} %all_to_all.36), calls=%async_computation | async-start | bytes 8192 | tf_op jit(solution)/shard_map/all_to_all | solution.py:68
  21.8 8.9 %all-to-all-start.1 = ((f32[8,1,256]{2,1,0:T(1,128)}), f32[8,1,256]{2,1,0:T(1,128)S(1)}, u32[]{:S(2)}, u32[]{:S(2)}) async-start(f32[8,1,256]{2,1,0:T(1,128)} %reshape.378), calls=%async_computation.1 | async-start | bytes 16384 | tf_op jit(solution)/shard_map/all_to_all | solution.py:65
  30.6 10.1 %all-to-all-start.3 = ((f32[8,32,128]{2,1,0:T(8,128)}), f32[8,32,128]{2,1,0:T(8,128)S(1)}, u32[]{:S(2)}, u32[]{:S(2)}) async-start(f32[8,32,128]{2,1,0:T(8,128)} %bitcast.10), calls=%async_computation.3 | async-start | bytes 262144 | tf_op jit(solution)/shard_map/all_to_all | solution.py:62
  48.7 9.8 %copy-start = (bf16[128,4096]{1,0:T(8,128)(2,1)S(1)}, bf16[128,4096]{1,0:T(8,128)(2,1)}, u32[]{:S(2)}) copy-start(bf16[128,4096]{1,0:T(8,128)(2,1)} %param.13) | copy-start | bytes 3145732
  54.2 51.8 %all-to-all-start.2 = ((bf16[4,64,4096]{2,1,0:T(8,128)(2,1)}), bf16[4,64,4096]{2,1,0:T(8,128)(2,1)S(1)}, u32[]{:S(2)}, u32[]{:S(2)}) async-start(bf16[4,64,4096]{2,1,0:T(8,128)(2,1)} %bitcast.5), calls=%async_computation.2 | async-start | bytes 4194304 | tf_op jit(solution)/shard_map/all_to_all | solution.py:95
  57.8 52.8 %copy-start.4 = (u32[32]{0:T(128)S(1)}, u32[32]{0:T(128)}, u32[]{:S(2)}) copy-start(u32[32]{0:T(128)} %constant.104) | copy-start | bytes 388
  106.0 52.2 %all-to-all-start.6 = ((bf16[4,64,4096]{2,1,0:T(8,128)(2,1)}), bf16[4,64,4096]{2,1,0:T(8,128)(2,1)}, u32[]{:S(2)}, u32[]{:S(2)}) async-start(bf16[4,64,4096]{2,1,0:T(8,128)(2,1)} %bitcast.17), calls=%async_computation.7 | async-start | bytes 4194304 | tf_op jit(solution)/shard_map/all_to_all | solution.py:96
  158.2 32.5 %copy-start.1 = (f32[256,768]{1,0:T(8,128)S(1)}, f32[256,768]{1,0:T(8,128)}, u32[]{:S(2)}) copy-start(f32[256,768]{1,0:T(8,128)} %fusion.10) | copy-start | bytes 2359300
  158.2 37.6 %slice-start = ((s8[6291456]{0:T(1024)(128)(4,1)}), s8[2097152]{0:T(1024)(128)(4,1)S(1)}, s32[]{:S(2)}) async-start(s8[6291456]{0:T(1024)(128)(4,1)} %bitcast.69), calls=%async_computation.13 | async-start | bytes 4194304
  171.2 8.7 %all-to-all-start.8 = ((bf16[4,1,64]{2,1,0:T(2,128)(2,1)}), bf16[4,1,64]{2,1,0:T(2,128)(2,1)S(1)}, u32[]{:S(2)}, u32[]{:S(2)}) async-start(bf16[4,1,64]{2,1,0:T(2,128)(2,1)} %convert_element_type.131), calls=%async_computation.10 | async-start | bytes 4096 | tf_op jit(solution)/shard_map/all_to_all | solution.py:140
  174.4 55.1 %reduce-scatter.6.cloned.1.call-start = ((), (), s32[]{:S(2)}) async-start(), calls=%async_computation.12 | async-start | bytes 3145728 | tf_op jit(solution)/shard_map/reduce_scatter | solution.py:127
  190.7 5.2 %slice-start.1 = ((s8[6291456]{0:T(1024)(128)(4,1)}), s8[4194304]{0:T(1024)(128)(4,1)S(1)}, s32[]{:S(2)}) async-start(s8[6291456]{0:T(1024)(128)(4,1)} %bitcast.69), calls=%async_computation.14 | async-start | bytes 8388608
  190.7 5.2 %copy-start.2 = (f32[256,768]{1,0:T(8,128)S(1)}, f32[256,768]{1,0:T(8,128)}, u32[]{:S(2)}) copy-start(f32[256,768]{1,0:T(8,128)} %fusion.6) | copy-start | bytes 2359300
  190.7 5.2 %copy-start.3 = (f32[256,768]{1,0:T(8,128)S(1)}, f32[256,768]{1,0:T(8,128)}, u32[]{:S(2)}) copy-start(f32[256,768]{1,0:T(8,128)} %get-tuple-element.14) | copy-start | bytes 2359300
  199.4 64.4 %reduce-scatter.4.cloned.1.call-start = ((), (), s32[]{:S(2)}) async-start(), calls=%async_computation.11 | async-start | bytes 3145728 | tf_op jit(solution)/shard_map/reduce_scatter | solution.py:124
  229.6 34.2 %all-to-all-start.7 = ((bf16[4,64,2048]{2,1,0:T(8,128)(2,1)}), bf16[4,64,2048]{2,1,0:T(8,128)(2,1)S(1)}, u32[]{:S(2)}, u32[]{:S(2)}) async-start(bf16[4,64,2048]{2,1,0:T(8,128)(2,1)} %bitcast.74), calls=%async_computation.9 | async-start | bytes 2097152 | tf_op jit(solution)/shard_map/all_to_all | solution.py:139
  263.8 30.3 %all-to-all-start.5 = ((bf16[4,64,2048]{2,1,0:T(8,128)(2,1)}), bf16[4,64,2048]{2,1,0:T(8,128)(2,1)S(1)}, u32[]{:S(2)}, u32[]{:S(2)}) async-start(bf16[4,64,2048]{2,1,0:T(8,128)(2,1)} %bitcast.73), calls=%async_computation.6 | async-start | bytes 2097152 | tf_op jit(solution)/shard_map/all_to_all | solution.py:138
Sparse Core Ops, SparseCore 0:
  199.5 30.0 reduce-scatter.5
  231.9 31.8 reduce-scatter.3
where the time goes:
time: 304 us; the launch traced here: 303 us
  waiting for transfers between devices  171 us (56%)
  starting transfers between devices  33.8 us (11%)
  matrix products  32.4 us (11%)
  local copies, waits for them, and re-layouts  28.3 us (9%)
  between operations  15 us (5%)
  blocking collectives  12.8 us (4%)
  other arithmetic  9.02 us (3%)
    all_to_all x1, waiting for transfers between devices, shards(): lax.all_to_all(pack(tokens), 'ep', split_axis=0, concat_axis=0, tiled=True)  43.8 us
    all_to_all x1, waiting for transfers between devices, shards(): lax.all_to_all(pack(masked_grad), 'ep', split_axis=0, concat_axis=0, tile...  36.1 us
    reduce_scatter x1, waiting for transfers between devices, shards(): lax.psum_scatter(out_terms.astype(jnp.bfloat16), 'tp', scatter_dimension=...  29.6 us
    reduce_scatter x1, waiting for transfers between devices, shards(): lax.psum_scatter(grad_terms.astype(jnp.bfloat16), 'tp', scatter_dimension...  24.1 us
    all_to_all x1, waiting for transfers between devices, shards(): lax.all_to_all(out_back, 'ep', split_axis=0, concat_axis=0, tiled=True)  22.9 us
    scatter x7, local copies, waits for them, and re-layouts, place_rows(): return buffer.at[target].set(values)  11.7 us
    all_to_all x1, blocking collectives, shards(): lax.all_to_all(pack(weight_b), 'ep', split_axis=0, concat_axis=0, tiled=T...  7.87 us
    gather x3, local copies, waits for them, and re-layouts, shards(): picked = jnp.take_along_axis(learner_logits, learner_routes, axis=1)  6.97 us
  transfers between devices with their start and end apart: 10, of which 9 were waited for; matrix products, arithmetic and copies ran while one was open for 11% of the time, Pallas kernels for 0%

commit v1 on v0

v1 whole, which is shorter than its diff:
```python
import functools

import jax
import jax.numpy as jnp
from jax import lax
from jax.experimental import pallas as pl
from jax.experimental.pallas import tpu as pltpu
from jax.sharding import PartitionSpec as P

MESH = pl.DeviceIdType.MESH
LANES = 128


def dot_nn(left, right):
    return jnp.dot(left, right, preferred_element_type=jnp.float32)


def dot_nt(left, right):
    return lax.dot_general(
        left, right, (((1,), (1,)), ((), ())), preferred_element_type=jnp.float32
    )


def layer_kernel(
    ep,
    tp,
    per,
    pack_ref,
    pack_grad_ref,
    unpack_ref,
    weight_ref,
    coef_ref,
    tokens_ref,
    grads_ref,
    gate_hbm,
    up_hbm,
    down_hbm,
    out_ref,
    token_grad_ref,
    router_ref,
    w_gate,
    w_up,
    w_down,
    tok_send,
    grad_send,
    tok_all,
    grad_all,
    pre_gate,
    pre_up,
    hidden,
    out_part,
    out_recv,
    out_back,
    out_home,
    tg_part,
    tg_recv,
    tg_back,
    tg_home,
    w_sem,
    z_send,
    z_recv,
    x_send,
    x_recv,
):
    share = tok_send.shape[2]
    z = lax.axis_index("ep")
    x = lax.axis_index("tp")

    def rows_of(index):
        return pl.ds(pl.multiple_of(index * per, per), per)

    def source(k):
        return lax.rem(z - k + ep, ep)

    def holder(k):
        return lax.rem(z + k, ep)

    barrier = pltpu.get_barrier_semaphore()
    for k in range(1, ep):
        pl.semaphore_signal(barrier, inc=1, device_id={"ep": holder(k)}, device_id_type=MESH)
    for j in range(1, tp):
        pl.semaphore_signal(
            barrier, inc=1, device_id={"tp": lax.rem(x + j, tp)}, device_id_type=MESH
        )

    w_copies = [
        pltpu.make_async_copy(gate_hbm.at[0], w_gate, w_sem.at[0]),
        pltpu.make_async_copy(up_hbm.at[0], w_up, w_sem.at[1]),
        pltpu.make_async_copy(down_hbm.at[0], w_down, w_sem.at[2]),
    ]
    for copy in w_copies:
        copy.start()

    def z_copy(kind, k):
        if kind < 2:
            sent, landed = ((tok_send, tok_all), (grad_send, grad_all))[kind]
            return pltpu.make_async_remote_copy(
                src_ref=sent.at[k],
                dst_ref=landed.at[x, rows_of(z)],
                send_sem=z_send.at[kind, k],
                recv_sem=z_recv.at[kind, k],
                device_id={"ep": holder(k)},
                device_id_type=MESH,
            )
        sent, landed = ((out_back, out_home), (tg_back, tg_home))[kind - 2]
        return pltpu.make_async_remote_copy(
            src_ref=sent.at[rows_of(source(k))],
            dst_ref=landed.at[rows_of(z)],
            send_sem=z_send.at[kind, k],
            recv_sem=z_recv.at[kind, k],
            device_id={"ep": source(k)},
            device_id_type=MESH,
        )

    def x_copy(kind, k, j):
        rows = rows_of(source(k))
        target = lax.rem(x + j, tp)
        if kind < 2:
            buffer = (tok_all, grad_all)[kind]
            sent, landed = buffer.at[x, rows], buffer.at[x, rows]
        else:
            part, recv = ((out_part, out_recv), (tg_part, tg_recv))[kind - 2]
            sent, landed = part.at[target, rows], recv.at[j - 1, rows]
        return pltpu.make_async_remote_copy(
            src_ref=sent,
            dst_ref=landed,
            send_sem=x_send.at[kind, k * tp + j],
            recv_sem=x_recv.at[kind, k * tp + j],
            device_id={"tp": target},
            device_id_type=MESH,
        )

    def x_start(kind, k):
        for j in range(1, tp):
            x_copy(kind, k, j).start()

    def x_wait_recv(kind, k):
        for j in range(1, tp):
            x_copy(kind, k, j).wait_recv()

    mine = pl.ds(pl.multiple_of(x * share, LANES), share)
    pl.semaphore_wait(barrier, ep - 1 + tp - 1)

    @pl.loop(1, ep)
    def _(k):
        packed = dot_nn(pack_ref[rows_of(holder(k)), :], tokens_ref[:, mine])
        tok_send[k] = packed.astype(jnp.bfloat16)
        z_copy(0, k).start()

    @pl.loop(0, tp)
    def _(h):
        lanes = pl.ds(pl.multiple_of(h * share, LANES), share)
        tok_all[h, rows_of(z), :] = dot_nn(
            pack_ref[rows_of(z), :], tokens_ref[:, lanes]
        ).astype(jnp.bfloat16)
        grad_all[h, rows_of(z), :] = dot_nn(
            pack_grad_ref[rows_of(z), :], grads_ref[:, lanes]
        ).astype(jnp.bfloat16)

    @pl.loop(1, ep)
    def _(k):
        packed = dot_nn(pack_grad_ref[rows_of(holder(k)), :], grads_ref[:, mine])
        grad_send[k] = packed.astype(jnp.bfloat16)

    def pump(kind, k):
        z_copy(kind, k).wait_recv()
        x_start(kind, k)
        if kind == 0:
            z_copy(1, k).start()

    def reduce_rows(kind, k):
        part, recv, back, home = (
            (out_part, out_recv, out_back, out_home),
            (tg_part, tg_recv, tg_back, tg_home),
        )[kind - 2]
        rows = rows_of(source(k))
        x_wait_recv(kind, k)
        total = part[x, rows, :].astype(jnp.float32)
        for j in range(1, tp):
            total = total + recv[j - 1, rows, :].astype(jnp.float32)
        total = total.astype(jnp.bfloat16)

        @pl.when(k == 0)
        def _():
            home[rows, :] = total

        @pl.when(k > 0)
        def _():
            back[rows, :] = total
            z_copy(kind, k).start()

    for copy in w_copies:
        copy.wait()

    @pl.loop(0, ep)
    def _(k):
        rows = rows_of(source(k))

        @pl.when((k >= 1) & (k + 1 < ep))
        def _():
            pump(0, k + 1)

        @pl.when(k >= 1)
        def _():
            x_wait_recv(0, k)

        gate = jnp.zeros((per, w_gate.shape[1]), jnp.float32)
        up = jnp.zeros((per, w_gate.shape[1]), jnp.float32)
        for h in range(tp):
            block = tok_all[h, rows, :]
            gate = gate + dot_nn(block, w_gate[h * share : (h + 1) * share, :])
            up = up + dot_nn(block, w_up[h * share : (h + 1) * share, :])
        pre_gate[rows, :] = gate
        pre_up[rows, :] = up
        hid = (gate * jax.nn.sigmoid(gate) * up).astype(jnp.bfloat16)
        hidden[rows, :] = hid
        for h in range(tp):
            out_part[h, rows, :] = dot_nn(
                hid, w_down[:, h * share : (h + 1) * share]
            ).astype(jnp.bfloat16)
        x_start(2, k)

        @pl.when(k == 0)
        def _():
            pump(0, k + 1)

    @pl.loop(0, ep)
    def _(k):
        rows = rows_of(source(k))

        @pl.when((k >= 1) & (k + 1 < ep))
        def _():
            pump(1, k + 1)

        @pl.when(k >= 1)
        def _():
            x_wait_recv(1, k)

        back = jnp.zeros((per, w_gate.shape[1]), jnp.float32)
        for h in range(tp):
            back = back + dot_nt(grad_all[h, rows, :], w_down[:, h * share : (h + 1) * share])
        gate = pre_gate[rows, :]
        up = pre_up[rows, :]
        sig = jax.nn.sigmoid(gate)
        score = jnp.sum(hidden[rows, :].astype(jnp.float32) * back, axis=1, keepdims=True)
        score = jnp.broadcast_to(score, (per, LANES)).astype(jnp.bfloat16)
        grad_up = (back * (gate * sig)).astype(jnp.bfloat16)
        grad_gate = (back * up * (sig * (1.0 + gate * (1.0 - sig)))).astype(jnp.bfloat16)
        for h in range(tp):
            cols = slice(h * share, (h + 1) * share)
            tg_part[h, rows, 0:share] = (
                dot_nt(grad_gate, w_gate[cols, :]) + dot_nt(grad_up, w_up[cols, :])
            ).astype(jnp.bfloat16)
            tg_part[h, rows, share : share + LANES] = score
        x_start(3, k)
        reduce_rows(2, k)

        @pl.when(k == 0)
        def _():
            pump(1, k + 1)

        @pl.when(k >= 1)
        def _():
            reduce_rows(3, k - 1)

    reduce_rows(3, jnp.int32(ep - 1))

    weight = weight_ref[...]

    @pl.loop(1, ep)
    def _(k):
        z_copy(2, k).wait_recv()

    out_ref[...] = (dot_nn(unpack_ref[...], out_home[...]) * weight).astype(jnp.bfloat16)

    @pl.loop(1, ep)
    def _(k):
        z_copy(3, k).wait_recv()

    token_grad_ref[...] = (
        dot_nn(unpack_ref[...], tg_home[:, 0:share]) * weight
    ).astype(jnp.bfloat16)
    router_ref[...] = (
        dot_nn(unpack_ref[...], tg_home[:, share : share + LANES]) * coef_ref[...]
    )

    for kind in range(4):

        @pl.loop(1, ep)
        def _(k):
            z_copy(kind, k).wait_send()

        @pl.loop(1 if kind < 2 else 0, ep)
        def _(k):
            for j in range(1, tp):
                x_copy(kind, k, j).wait_send()


def shards(logits, routes, owner, tokens, out_grad, resp_lengths, w_gate, w_up, w_down):
    tok_count, width = tokens.shape
    top = routes.shape[1]
    ep = lax.axis_size("ep")
    tp = lax.axis_size("tp")
    sp = lax.axis_size("sp")
    owner_count = ep * sp
    local_count = w_gate.shape[0]
    assert local_count == 1
    hidden_width = w_gate.shape[2]
    per = 2 * tok_count // ep
    slots = ep * per
    share = width // tp
    me = lax.axis_index("ep") * sp + lax.axis_index("sp")

    columns = jnp.arange(logits.shape[1], dtype=jnp.int32)
    hits = routes[:, :, None] == columns[None, None, :]
    picked = jnp.sum(jnp.where(hits, logits[:, None, :], 0.0), axis=2)
    highest = jnp.max(picked, axis=1, keepdims=True)
    raised = jnp.exp(picked - highest)
    gates = raised / jnp.sum(raised, axis=1, keepdims=True)
    table = jnp.concatenate(
        [
            gates.T,
            routes.astype(jnp.float32).T,
            owner.astype(jnp.float32)[None, :],
            jnp.zeros((24 - 2 * top - 1, tok_count), jnp.float32),
        ],
        axis=0,
    )
    everyone = lax.all_gather(table, ("ep", "sp"), axis=1, tiled=True)
    positions = jnp.arange(tok_count, dtype=jnp.float32) + (me * tok_count).astype(jnp.float32)
    chosen = (everyone[2 * top][:, None] == positions[None, :]).astype(jnp.float32)
    mine = jnp.dot(everyone, chosen, precision=lax.Precision.HIGHEST)
    gate_rows = mine[:top]
    route_rows = mine[top : 2 * top]
    in_window = route_rows < ep
    expert_ids = jnp.sum(jnp.where(in_window, route_rows, 0.0), axis=0)
    weight = jnp.sum(jnp.where(in_window, gate_rows, 0.0), axis=0)
    steps = jnp.arange(tok_count, dtype=jnp.int32)
    live = steps < resp_lengths[0]
    same = (expert_ids[:, None] == expert_ids[None, :]) & (steps[:, None] < steps[None, :])
    rank = jnp.sum(same.astype(jnp.float32), axis=0)
    slot = expert_ids * per + rank
    slot_line = jnp.arange(slots, dtype=jnp.float32)
    pack = slot_line[:, None] == slot[None, :]
    pack_grad = (pack & live[None, :]).astype(jnp.bfloat16)
    unpack = (slot[:, None] == slot_line[None, :]).astype(jnp.bfloat16)
    pack = pack.astype(jnp.bfloat16)
    spread = jnp.where(in_window, 1.0, 0.0) - gate_rows
    coef = (
        jnp.sum(
            jnp.where(
                route_rows[:, :, None] == columns.astype(jnp.float32)[None, None, :],
                spread[:, :, None],
                0.0,
            ),
            axis=0,
        )
        * weight[:, None]
    )
    weight_b = weight.astype(jnp.bfloat16).astype(jnp.float32)
    weight_col = jnp.broadcast_to(weight_b[:, None], (tok_count, LANES))[:, :1]

    vmem = pl.BlockSpec(memory_space=pltpu.VMEM)
    anywhere = pl.BlockSpec(memory_space=pl.ANY)
    bf16 = jnp.bfloat16
    return pl.pallas_call(
        functools.partial(layer_kernel, ep, tp, per),
        out_shape=(
            jax.ShapeDtypeStruct((tok_count, share), bf16),
            jax.ShapeDtypeStruct((tok_count, share), bf16),
            jax.ShapeDtypeStruct((tok_count, logits.shape[1]), jnp.float32),
        ),
        in_specs=[vmem] * 7 + [anywhere] * 3,
        out_specs=(vmem, vmem, vmem),
        scratch_shapes=[
            pltpu.VMEM((width, hidden_width), bf16),
            pltpu.VMEM((width, hidden_width), bf16),
            pltpu.VMEM((hidden_width, width), bf16),
            pltpu.VMEM((ep, per, share), bf16),
            pltpu.VMEM((ep, per, share), bf16),
            pltpu.VMEM((tp, slots, share), bf16),
            pltpu.VMEM((tp, slots, share), bf16),
            pltpu.VMEM((slots, hidden_width), jnp.float32),
            pltpu.VMEM((slots, hidden_width), jnp.float32),
            pltpu.VMEM((slots, hidden_width), bf16),
            pltpu.VMEM((tp, slots, share), bf16),
            pltpu.VMEM((tp - 1, slots, share), bf16),
            pltpu.VMEM((slots, share), bf16),
            pltpu.VMEM((slots, share), bf16),
            pltpu.VMEM((tp, slots, share + LANES), bf16),
            pltpu.VMEM((tp - 1, slots, share + LANES), bf16),
            pltpu.VMEM((slots, share + LANES), bf16),
            pltpu.VMEM((slots, share + LANES), bf16),
            pltpu.SemaphoreType.DMA((3,)),
            pltpu.SemaphoreType.DMA((4, ep)),
            pltpu.SemaphoreType.DMA((4, ep)),
            pltpu.SemaphoreType.DMA((4, ep * tp)),
            pltpu.SemaphoreType.DMA((4, ep * tp)),
        ],
        compiler_params=pltpu.CompilerParams(
            collective_id=0, has_side_effects=True, vmem_limit_bytes=56 * 1024 * 1024
        ),
        cost_estimate=pl.CostEstimate(
            flops=12 * slots * width * hidden_width,
            bytes_accessed=6 * width * hidden_width + 6 * tok_count * width,
            transcendentals=2 * slots * hidden_width,
        ),
        name="expert_layer",
    )(
        pack,
        pack_grad,
        unpack,
        weight_col,
        coef,
        tokens,
        out_grad,
        w_gate,
        w_up,
        w_down,
    )


def solution(mesh):
    in_specs = (
        P(("groups", "ep", "sp"), None),
        P(("groups", "ep", "sp"), None),
        P(("groups", "ep", "sp")),
        P(("groups", "ep", "sp"), None),
        P(("groups", "ep", "sp"), None),
        P(("groups", "ep", "sp")),
        P("ep", None, "tp"),
        P("ep", None, "tp"),
        P("ep", "tp", None),
    )
    out_specs = (
        P(("groups", "ep", "sp"), "tp"),
        P(("groups", "ep", "sp"), "tp"),
        P(("groups", "ep", "sp"), None),
    )
    return jax.shard_map(shards, mesh=mesh, in_specs=in_specs, out_specs=out_specs, check_vma=False)
```

time: 304 us -> 151 us (0.50)
  waiting for transfers between devices: 171 us -> 0 us
  Pallas kernels: 0 us -> 121 us
  starting transfers between devices: 33.8 us -> 0 us
  matrix products: 32.4 us -> 0.39 us
  local copies, waits for them, and re-layouts: 28.3 us -> 6.88 us
  between operations: 15 us -> 1.35 us
  other arithmetic: 9.02 us -> 5.58 us
    pallas_call x0 -> x1, Pallas kernels: none -> 121 us  [shards(): pl.pallas_call(functools.partial(layer_kernel, ep, tp, per), out_shape=(j...]
    all_to_all x8 -> x0, waiting for transfers between devices: 118 us -> none  [the longest x1 43.8 us: shards(): lax.all_to_all(pack(tokens), 'ep', split_axis=0, concat_axis=0, tiled=True)]
    reduce_scatter x2 -> x0, waiting for transfers between devices: 53.7 us -> none  [the longest x1 29.6 us: shards(): lax.psum_scatter(out_terms.astype(jnp.bfloat16), 'tp', scatter_dimension=...]
    all_to_all x8 -> x0, starting transfers between devices: 33.7 us -> none  [the longest x1 6.33 us: shards(): lax.all_to_all(send_rows(arrival_values, -1.0), ('ep', 'sp'), split_axis=...]
    dot_general x6 -> x1, matrix products: 32.4 us -> 0.39 us  [shards(): mine = jnp.dot(everyone, chosen, precision=lax.Precision.HIGHEST)]
    all_gather x0 -> x1, blocking collectives: none -> 15.6 us  [shards(): everyone = lax.all_gather(table, ('ep', 'sp'), axis=1, tiled=True)]
    scatter x7 -> x0, local copies, waits for them, and re-layouts: 11.7 us -> none  [place_rows(): return buffer.at[target].set(values)]
    gather x6 -> x0, local copies, waits for them, and re-layouts: 11.6 us -> none  [the longest x3 6.97 us: shards(): picked = jnp.take_along_axis(learner_logits, learner_routes, axis=1)]
  transfers between devices with their start and end apart: 10 -> 0, of which waited for: 9 -> 0; matrix products, arithmetic and copies ran while one was open for 11% -> 0% of each run, Pallas kernels for 0% -> 0%
where the time goes in v1:
time: 151 us; the launch traced here: 150 us
  Pallas kernels  121 us (80%)
  blocking collectives  15.6 us (10%)
  local copies, waits for them, and re-layouts  6.88 us (5%)
  other arithmetic  5.58 us (4%)
    pallas_call x1, Pallas kernels, shards(): pl.pallas_call(functools.partial(layer_kernel, ep, tp, per), out_shape=(j...  121 us
    all_gather x1, blocking collectives, shards(): everyone = lax.all_gather(table, ('ep', 'sp'), axis=1, tiled=True)  15.6 us
    unnamed x4, local copies, waits for them, and re-layouts  6.02 us

profile of v1, /device:TPU:0, one launch (start us, length us, event | category | flops | bytes accessed | tf_op | source)
XLA Modules:
  0.0 150.4 jit_solution(3013022005099617790)
XLA Ops:
  1.3 0.7 convert_bitcast_fusion.1
  2.0 0.1 pad.3.clone
  2.1 0.7 convert_bitcast_fusion
  2.7 0.8 copy.22
  3.5 1.2 select_reduce_fusion.1
  4.7 0.1 reduce_max.9
  4.8 0.2 fusion.9
  5.0 0.1 divide_bitcast_fusion
  5.2 0.1 maximum_maximum_fusion
  5.3 15.6 %all_gather.3 = f32[24,1024]{1,0:T(8,128)S(1)} all-gather(f32[24,128]{1,0:T(8,128)S(1)} %maximum_maximum_fusion), channel_id=1, replica_groups=mesh['groups'=2,'ep'=4,'tp'=2,'sp'=2] {'ep','sp'}, dimensions={1}, use_global_device_ids=true | all-gather | bytes 110592 | tf_op jit(solution)/shard_map/all_gather | solution.py:329
  20.9 0.4 fusion
  21.3 0.3 select_reduce_fusion
  21.7 0.7 convert_reduce_fusion
  22.4 0.7 copy.24.weight_ref
  23.1 0.7 fusion.7.unpack_ref
  23.8 0.7 fusion.6
  24.6 120.6 %expert_layer.1 = (bf16[128,2048]{1,0:T(8,128)(2,1)}, bf16[128,2048]{1,0:T(8,128)(2,1)}, f32[128,128]{1,0:T(8,128)}) custom-call(bf16[256,128]{1,0:T(8,128)(2,1)} %get-tuple-element.9.pack_ref, bf16[256,128]{1,0:T(8,128)(2,1)} %get-tuple-element.8.pack_grad_ref, bf16[128,256]{1,0:T(8,128)(2,1)} %fusion.7.unpack_ref, f32[128,1]{1,0:T(8,128)} %copy.24.weight_ref, ...), custom_call_target="tpu_custom_call" | custom-call | flops 9663676416 | bytes 22020096 | tf_op jit(solution)/shard_map/expert_layer/pallas_call | solution.py:366
  145.1 1.9 %copy.29 = bf16[128,2048]{1,0:T(8,128)(2,1)} copy(bf16[128,2048]{1,0:T(8,128)(2,1)} %get-tuple-element.15) | data formatting | bytes 1048576
  147.0 1.9 %copy.30 = bf16[128,2048]{1,0:T(8,128)(2,1)} copy(bf16[128,2048]{1,0:T(8,128)(2,1)} %get-tuple-element.16) | data formatting | bytes 1048576
  148.9 1.5 copy.31
  (10 shorter events, 0.1 us)

commit v2 on v1

v2 whole, which is shorter than its diff:
```python
import functools

import jax
import jax.numpy as jnp
from jax import lax
from jax.experimental import pallas as pl
from jax.experimental.pallas import tpu as pltpu
from jax.sharding import PartitionSpec as P

MESH = pl.DeviceIdType.MESH
LANES = 128


def dot_nn(left, right):
    return jnp.dot(left, right, preferred_element_type=jnp.float32)


def dot_nt(left, right):
    return lax.dot_general(
        left, right, (((1,), (1,)), ((), ())), preferred_element_type=jnp.float32
    )


def layer_kernel(
    ep,
    tp,
    sp,
    per,
    logits_ref,
    routes_ref,
    owner_ref,
    length_ref,
    tokens_hbm,
    grads_hbm,
    gate_hbm,
    up_hbm,
    down_hbm,
    out_ref,
    token_grad_ref,
    router_ref,
    table,
    pack_ref,
    pack_grad_ref,
    unpack_ref,
    tokens_ref,
    grads_ref,
    w_gate,
    w_up,
    w_down,
    tok_send,
    grad_send,
    tok_near,
    grad_near,
    tok_all,
    grad_all,
    pre_gate,
    pre_up,
    hidden,
    out_part,
    out_recv,
    out_back,
    out_home,
    tg_part,
    tg_recv,
    tg_back,
    tg_home,
    w_sem,
    t_send,
    t_recv,
    z_send,
    z_recv,
    x_send,
    x_recv,
):
    share = tok_send.shape[2]
    tok_count = tokens_ref.shape[0]
    slots = ep * per
    top = routes_ref.shape[1]
    owner_count = ep * sp
    z = lax.axis_index("ep")
    x = lax.axis_index("tp")
    me = z * sp + lax.axis_index("sp")

    def rows_of(index):
        return pl.ds(pl.multiple_of(index * per, per), per)

    def peer(k):
        k = jnp.int32(k)
        both = 0
        bit = 1
        while bit < ep:
            both = both + bit * (lax.rem(lax.div(z, bit), 2) * lax.rem(lax.div(k, bit), 2))
            bit *= 2
        return z + k - 2 * both

    def owner_at(o):
        other = lax.rem(me + o, owner_count)
        return {"ep": lax.div(other, sp), "sp": lax.rem(other, sp)}

    barrier = pltpu.get_barrier_semaphore()

    @pl.loop(1, owner_count)
    def _(o):
        pl.semaphore_signal(barrier, inc=1, device_id=owner_at(o), device_id_type=MESH)

    for j in range(1, tp):
        pl.semaphore_signal(
            barrier, inc=1, device_id={"tp": lax.rem(x + j, tp)}, device_id_type=MESH
        )

    in_copies = [
        pltpu.make_async_copy(tokens_hbm, tokens_ref, w_sem.at[3]),
        pltpu.make_async_copy(grads_hbm, grads_ref, w_sem.at[4]),
    ]
    w_copies = [
        pltpu.make_async_copy(gate_hbm.at[0], w_gate, w_sem.at[0]),
        pltpu.make_async_copy(up_hbm.at[0], w_up, w_sem.at[1]),
        pltpu.make_async_copy(down_hbm.at[0], w_down, w_sem.at[2]),
    ]
    for copy in in_copies + w_copies:
        copy.start()

    square = (tok_count, tok_count)
    line = lax.broadcasted_iota(jnp.int32, square, 1)
    column = lax.broadcasted_iota(jnp.int32, square, 0)
    lanes = lax.broadcasted_iota(jnp.int32, logits_ref.shape, 1)
    logits = logits_ref[...]
    routes = routes_ref[...]
    picked = jnp.full(logits.shape, -1e30, jnp.float32)
    named = jnp.zeros(logits.shape, jnp.float32)
    for j in range(top):
        route = routes[:, j : j + 1]
        value = jnp.sum(jnp.where(lanes == route, logits, 0.0), axis=1, keepdims=True)
        picked = jnp.where(lanes == j, value, picked)
        named = jnp.where(lanes == top + j, route.astype(jnp.float32), named)
    raised = jnp.where(
        lanes < top, jnp.exp(picked - jnp.max(picked, axis=1, keepdims=True)), 0.0
    )
    merged = raised / jnp.sum(raised, axis=1, keepdims=True) + named
    table[me, 0 : 2 * top, :] = merged.T[0 : 2 * top, :]
    table[me, 2 * top : 3 * top, :] = jnp.broadcast_to(
        owner_ref[...].astype(jnp.float32), (top, tok_count)
    )

    def table_copy(o):
        return pltpu.make_async_remote_copy(
            src_ref=table.at[me],
            dst_ref=table.at[me],
            send_sem=t_send.at[o],
            recv_sem=t_recv.at[o],
            device_id=owner_at(o),
            device_id_type=MESH,
        )

    pl.semaphore_wait(barrier, owner_count - 1 + tp - 1)

    @pl.loop(1, owner_count)
    def _(o):
        table_copy(o).start()

    base = (me * tok_count).astype(jnp.float32)
    position = column.astype(jnp.float32) + base

    @pl.loop(1, owner_count)
    def _(o):
        table_copy(o).wait_recv()

    def gather(o, found):
        block = table[o]
        chosen = jnp.where(position == block[2 * top : 2 * top + 1, :], 1.0, 0.0)
        return found + lax.dot_general(
            chosen,
            block,
            (((1,), (1,)), ((), ())),
            precision=lax.Precision.HIGHEST,
            preferred_element_type=jnp.float32,
        )

    found = lax.fori_loop(
        0, owner_count, gather, jnp.zeros((tok_count, 3 * top), jnp.float32)
    )
    gate_rows = found[:, 0:top]
    route_rows = jnp.floor(found[:, top : 2 * top] + 0.5)
    inside = route_rows < ep
    expert = jnp.sum(jnp.where(inside, route_rows, 0.0), axis=1, keepdims=True)
    weight = jnp.sum(jnp.where(inside, gate_rows, 0.0), axis=1, keepdims=True)
    expert_square = jnp.broadcast_to(expert, square)
    same = (expert_square == expert_square.T) & (line < column)
    rank = jnp.sum(jnp.where(same, 1.0, 0.0), axis=1, keepdims=True)
    slot = expert * per + rank
    slot_line = jnp.broadcast_to(slot, square).T[0:1, :]
    slot_rows = lax.broadcasted_iota(jnp.int32, (slots, tok_count), 0).astype(jnp.float32)
    one_hot = jnp.where(slot_rows == slot_line, 1.0, 0.0)
    pack_ref[...] = one_hot.astype(jnp.bfloat16)
    live = line[0:1, :] < length_ref[...]
    pack_grad_ref[...] = jnp.where(live, one_hot, 0.0).astype(jnp.bfloat16)

    def slab(source_ref, placed, where, h):
        cols = pl.ds(pl.multiple_of(h * share, LANES), share)
        return dot_nn(placed[rows_of(where), :], source_ref[:, cols]).astype(jnp.bfloat16)

    def z_copy(kind, k):
        if kind < 2:
            sent, landed = ((tok_send, tok_all), (grad_send, grad_all))[kind]
            source, target = sent.at[k], landed.at[x, rows_of(z)]
        else:
            sent, landed = ((out_back, out_home), (tg_back, tg_home))[kind - 2]
            source, target = sent.at[rows_of(peer(k))], landed.at[rows_of(z)]
        return pltpu.make_async_remote_copy(
            src_ref=source,
            dst_ref=target,
            send_sem=z_send.at[kind, k],
            recv_sem=z_recv.at[kind, k],
            device_id={"ep": peer(k)},
            device_id_type=MESH,
        )

    def near_copy(kind):
        sent, landed = ((tok_near, tok_all), (grad_near, grad_all))[kind]
        return pltpu.make_async_remote_copy(
            src_ref=sent,
            dst_ref=landed.at[:, rows_of(z)],
            send_sem=z_send.at[kind, 1],
            recv_sem=z_recv.at[kind, 1],
            device_id={"ep": peer(1)},
            device_id_type=MESH,
        )

    def x_copy(kind, k, j):
        rows = rows_of(peer(k))
        target = lax.rem(x + j, tp)
        if kind < 2:
            buffer = (tok_all, grad_all)[kind]
            sent, landed = buffer.at[x, rows], buffer.at[x, rows]
        else:
            part, recv = ((out_part, out_recv), (tg_part, tg_recv))[kind - 2]
            sent, landed = part.at[target, rows], recv.at[j - 1, rows]
        return pltpu.make_async_remote_copy(
            src_ref=sent,
            dst_ref=landed,
            send_sem=x_send.at[kind, k * tp + j],
            recv_sem=x_recv.at[kind, k * tp + j],
            device_id={"tp": target},
            device_id_type=MESH,
        )

    def x_start(kind, k):
        for j in range(1, tp):
            x_copy(kind, k, j).start()

    def x_wait_recv(kind, k):
        for j in range(1, tp):
            x_copy(kind, k, j).wait_recv()

    in_copies[0].wait()

    @pl.loop(2, ep)
    def _(k):
        tok_send[k] = slab(tokens_ref, pack_ref, peer(k), x)
        z_copy(0, k).start()

    @pl.loop(0, tp)
    def _(h):
        tok_near[h] = slab(tokens_ref, pack_ref, peer(1), h)

    near_copy(0).start()

    @pl.loop(0, tp)
    def _(h):
        tok_all[h, rows_of(z), :] = slab(tokens_ref, pack_ref, z, h)

    in_copies[1].wait()

    @pl.loop(2, ep)
    def _(k):
        grad_send[k] = slab(grads_ref, pack_grad_ref, peer(k), x)

    @pl.loop(0, tp)
    def _(h):
        grad_near[h] = slab(grads_ref, pack_grad_ref, peer(1), h)
        grad_all[h, rows_of(z), :] = slab(grads_ref, pack_grad_ref, z, h)

    slot_columns = lax.broadcasted_iota(jnp.int32, (tok_count, slots), 1).astype(jnp.float32)
    unpack_ref[...] = jnp.where(slot_columns == slot, 1.0, 0.0).astype(jnp.bfloat16)
    coef = jnp.zeros(logits.shape, jnp.float32)
    spread = jnp.where(inside, 1.0, 0.0) - gate_rows
    lane_values = lanes.astype(jnp.float32)
    for j in range(top):
        coef = coef + jnp.where(
            lane_values == route_rows[:, j : j + 1], spread[:, j : j + 1], 0.0
        )
    router_ref[...] = coef * weight
    weight = weight.astype(jnp.bfloat16).astype(jnp.float32)

    def pump(kind, k):
        z_copy(kind, k).wait_recv()
        x_start(kind, k)
        if kind == 0:
            z_copy(1, k).start()

    def reduce_rows(kind, k):
        part, recv, back, home = (
            (out_part, out_recv, out_back, out_home),
            (tg_part, tg_recv, tg_back, tg_home),
        )[kind - 2]
        rows = rows_of(peer(k))
        x_wait_recv(kind, k)
        total = part[x, rows, :].astype(jnp.float32)
        for j in range(1, tp):
            total = total + recv[j - 1, rows, :].astype(jnp.float32)
        total = total.astype(jnp.bfloat16)

        @pl.when(k == 0)
        def _():
            home[rows, :] = total

        @pl.when(k > 0)
        def _():
            back[rows, :] = total
            z_copy(kind, k).start()

    for copy in w_copies:
        copy.wait()

    @pl.loop(0, ep)
    def _(k):
        rows = rows_of(peer(k))

        @pl.when((k >= 1) & (k + 1 < ep))
        def _():
            pump(0, k + 1)

        @pl.when(k == 1)
        def _():
            near_copy(0).wait_recv()
            near_copy(1).start()

        @pl.when(k >= 2)
        def _():
            x_wait_recv(0, k)

        gate = jnp.zeros((per, w_gate.shape[1]), jnp.float32)
        up = jnp.zeros((per, w_gate.shape[1]), jnp.float32)
        for h in range(tp):
            block = tok_all[h, rows, :]
            gate = gate + dot_nn(block, w_gate[h * share : (h + 1) * share, :])
            up = up + dot_nn(block, w_up[h * share : (h + 1) * share, :])
        pre_gate[rows, :] = gate
        pre_up[rows, :] = up
        hid = (gate * jax.nn.sigmoid(gate) * up).astype(jnp.bfloat16)
        hidden[rows, :] = hid
        for h in range(tp):
            out_part[h, rows, :] = dot_nn(
                hid, w_down[:, h * share : (h + 1) * share]
            ).astype(jnp.bfloat16)
        x_start(2, k)

    @pl.loop(0, ep)
    def _(k):
        rows = rows_of(peer(k))
        reduce_rows(2, lax.rem(k + 2, ep))

        @pl.when(k + 2 < ep)
        def _():
            pump(1, k + 2)

        @pl.when(k == 1)
        def _():
            near_copy(1).wait_recv()

        @pl.when(k >= 2)
        def _():
            x_wait_recv(1, k)

        back = jnp.zeros((per, w_gate.shape[1]), jnp.float32)
        for h in range(tp):
            back = back + dot_nt(grad_all[h, rows, :], w_down[:, h * share : (h + 1) * share])
        gate = pre_gate[rows, :]
        up = pre_up[rows, :]
        sig = jax.nn.sigmoid(gate)
        score = jnp.sum(hidden[rows, :].astype(jnp.float32) * back, axis=1, keepdims=True)
        score = jnp.broadcast_to(score, (per, LANES)).astype(jnp.bfloat16)
        grad_up = (back * (gate * sig)).astype(jnp.bfloat16)
        grad_gate = (back * up * (sig * (1.0 + gate * (1.0 - sig)))).astype(jnp.bfloat16)
        for h in range(tp):
            cols = slice(h * share, (h + 1) * share)
            tg_part[h, rows, 0:share] = (
                dot_nt(grad_gate, w_gate[cols, :]) + dot_nt(grad_up, w_up[cols, :])
            ).astype(jnp.bfloat16)
            tg_part[h, rows, share : share + LANES] = score
        x_start(3, k)

        @pl.when(k >= 1)
        def _():
            reduce_rows(3, k - 1)

    reduce_rows(3, jnp.int32(ep - 1))

    @pl.loop(1, ep)
    def _(k):
        z_copy(2, k).wait_recv()

    out_ref[...] = (dot_nn(unpack_ref[...], out_home[...]) * weight).astype(jnp.bfloat16)

    @pl.loop(1, ep)
    def _(k):
        z_copy(3, k).wait_recv()

    token_grad_ref[...] = (
        dot_nn(unpack_ref[...], tg_home[:, 0:share]) * weight
    ).astype(jnp.bfloat16)
    router_ref[...] = router_ref[...] * dot_nn(
        unpack_ref[...], tg_home[:, share : share + LANES]
    )

    @pl.loop(1, owner_count)
    def _(o):
        table_copy(o).wait_send()

    for kind in range(4):
        if kind < 2:
            near_copy(kind).wait_send()

        @pl.loop(2 if kind < 2 else 1, ep)
        def _(k):
            z_copy(kind, k).wait_send()

        @pl.loop(2 if kind < 2 else 0, ep)
        def _(k):
            for j in range(1, tp):
                x_copy(kind, k, j).wait_send()


def copy_kernel(a_in, b_in, c_in, a_out, b_out, c_out, sem):
    copies = [
        pltpu.make_async_copy(source, target, sem.at[i])
        for i, (source, target) in enumerate(((a_in, a_out), (b_in, b_out), (c_in, c_out)))
    ]
    for copy in copies:
        copy.start()
    for copy in copies:
        copy.wait()


def shards(logits, routes, owner, tokens, out_grad, resp_lengths, w_gate, w_up, w_down):
    tok_count, width = tokens.shape
    top = routes.shape[1]
    ep = lax.axis_size("ep")
    tp = lax.axis_size("tp")
    sp = lax.axis_size("sp")
    owner_count = ep * sp
    assert w_gate.shape[0] == 1 and ep >= 4 and ep & (ep - 1) == 0
    hidden_width = w_gate.shape[2]
    per = 2 * tok_count // ep
    slots = ep * per
    share = width // tp
    vmem = pl.BlockSpec(memory_space=pltpu.VMEM)
    anywhere = pl.BlockSpec(memory_space=pl.ANY)
    bf16 = jnp.bfloat16
    out_shape = (
        jax.ShapeDtypeStruct((tok_count, share), bf16),
        jax.ShapeDtypeStruct((tok_count, share), bf16),
        jax.ShapeDtypeStruct((tok_count, logits.shape[1]), jnp.float32),
    )
    results = pl.pallas_call(
        functools.partial(layer_kernel, ep, tp, sp, per),
        out_shape=out_shape,
        in_specs=[vmem] * 4 + [anywhere] * 5,
        out_specs=(vmem, vmem, vmem),
        scratch_shapes=[
            pltpu.VMEM((owner_count, 3 * top, tok_count), jnp.float32),
            pltpu.VMEM((slots, tok_count), bf16),
            pltpu.VMEM((slots, tok_count), bf16),
            pltpu.VMEM((tok_count, slots), bf16),
            pltpu.VMEM((tok_count, width), bf16),
            pltpu.VMEM((tok_count, width), bf16),
            pltpu.VMEM((width, hidden_width), bf16),
            pltpu.VMEM((width, hidden_width), bf16),
            pltpu.VMEM((hidden_width, width), bf16),
            pltpu.VMEM((ep, per, share), bf16),
            pltpu.VMEM((ep, per, share), bf16),
            pltpu.VMEM((tp, per, share), bf16),
            pltpu.VMEM((tp, per, share), bf16),
            pltpu.VMEM((tp, slots, share), bf16),
            pltpu.VMEM((tp, slots, share), bf16),
            pltpu.VMEM((slots, hidden_width), jnp.float32),
            pltpu.VMEM((slots, hidden_width), jnp.float32),
            pltpu.VMEM((slots, hidden_width), bf16),
            pltpu.VMEM((tp, slots, share), bf16),
            pltpu.VMEM((tp - 1, slots, share), bf16),
            pltpu.VMEM((slots, share), bf16),
            pltpu.VMEM((slots, share), bf16),
            pltpu.VMEM((tp, slots, share + LANES), bf16),
            pltpu.VMEM((tp - 1, slots, share + LANES), bf16),
            pltpu.VMEM((slots, share + LANES), bf16),
            pltpu.VMEM((slots, share + LANES), bf16),
            pltpu.SemaphoreType.DMA((5,)),
            pltpu.SemaphoreType.DMA((owner_count,)),
            pltpu.SemaphoreType.DMA((owner_count,)),
            pltpu.SemaphoreType.DMA((4, ep)),
            pltpu.SemaphoreType.DMA((4, ep)),
            pltpu.SemaphoreType.DMA((4, ep * tp)),
            pltpu.SemaphoreType.DMA((4, ep * tp)),
        ],
        compiler_params=pltpu.CompilerParams(
            collective_id=0, has_side_effects=True, vmem_limit_bytes=56 * 1024 * 1024
        ),
        cost_estimate=pl.CostEstimate(
            flops=12 * slots * width * hidden_width,
            bytes_accessed=6 * width * hidden_width + 6 * tok_count * width,
            transcendentals=2 * slots * hidden_width,
        ),
        name="expert_layer",
    )(
        logits,
        routes,
        owner.reshape(1, tok_count),
        resp_lengths.reshape(1, 1),
        tokens,
        out_grad,
        w_gate,
        w_up,
        w_down,
    )
    return pl.pallas_call(
        copy_kernel,
        out_shape=out_shape,
        in_specs=[anywhere] * 3,
        out_specs=(anywhere,) * 3,
        scratch_shapes=[pltpu.SemaphoreType.DMA((3,))],
        name="hand_over",
    )(*results)


def solution(mesh):
    in_specs = (
        P(("groups", "ep", "sp"), None),
        P(("groups", "ep", "sp"), None),
        P(("groups", "ep", "sp")),
        P(("groups", "ep", "sp"), None),
        P(("groups", "ep", "sp"), None),
        P(("groups", "ep", "sp")),
        P("ep", None, "tp"),
        P("ep", None, "tp"),
        P("ep", "tp", None),
    )
    out_specs = (
        P(("groups", "ep", "sp"), "tp"),
        P(("groups", "ep", "sp"), "tp"),
        P(("groups", "ep", "sp"), None),
    )
    return jax.shard_map(shards, mesh=mesh, in_specs=in_specs, out_specs=out_specs, check_vma=False)
```

time: 151 us -> 157 us (1.040)
  Pallas kernels: 121 us -> 153 us
  blocking collectives: 15.6 us -> 0 us
  other arithmetic: 5.58 us -> 0 us
  local copies, waits for them, and re-layouts: 6.88 us -> 1.42 us
    pallas_call x1 -> x2, Pallas kernels: 121 us -> 153 us  [the longest x1 118 us: shards(): pl.pallas_call(functools.partial(layer_kernel, ep, tp, sp, per), out_shap...]
    all_gather x1 -> x0, blocking collectives: 15.6 us -> none  [shards(): everyone = lax.all_gather(table, ('ep', 'sp'), axis=1, tiled=True)]
    unnamed x4 -> x1, local copies, waits for them, and re-layouts: 6.02 us -> 1.42 us
    reduce_sum x5 -> x0, other arithmetic: 2.48 us -> none  [the longest x1 1.2 us: shards(): picked = jnp.sum(jnp.where(hits, logits[:, None, :], 0.0), axis=2)]
where the time goes in v2:
time: 157 us; the launch traced here: 156 us
  Pallas kernels  153 us (97%)
    pallas_call x1, Pallas kernels, shards(): pl.pallas_call(functools.partial(layer_kernel, ep, tp, sp, per), out_shap...  118 us
    pallas_call x1, Pallas kernels, shards(): pl.pallas_call(copy_kernel, out_shape=out_shape, in_specs=[anywhere] * 3,...  34.9 us

profile of v2, /device:TPU:0, one launch (start us, length us, event | category | flops | bytes accessed | tf_op | source)
XLA Modules:
  0.0 155.9 jit_solution(10860251840614516702)
XLA Ops:
  1.3 1.4 copy.12.routes_ref
  2.7 118.4 %expert_layer.1 = (bf16[128,2048]{1,0:T(8,128)(2,1)}, bf16[128,2048]{1,0:T(8,128)(2,1)}, f32[128,128]{1,0:T(8,128)}) custom-call(f32[128,128]{1,0:T(8,128)} %logits_ref.1, s32[128,8]{1,0:T(8,128)} %copy.12.routes_ref, s32[1,128]{1,0:T(1,128)} %bitcast.3, s32[1,1]{1,0:T(1,128)} %bitcast.2.length_ref, bf16[128,4096]{1,0:T(8,128)(2,1)} %tokens_hbm.1, ...), custom_call_target="tpu_custom_call" | custom-call | flops 9663676416 | bytes 22020096 | tf_op jit(solution)/shard_map/expert_layer/pallas_call | solution.py:465
  121.1 34.9 %hand_over.1 = (bf16[128,2048]{1,0:T(8,128)(2,1)}, bf16[128,2048]{1,0:T(8,128)(2,1)}, f32[128,128]{1,0:T(8,128)}) custom-call(bf16[128,2048]{1,0:T(8,128)(2,1)} %get-tuple-element.6.a_in, bf16[128,2048]{1,0:T(8,128)(2,1)} %get-tuple-element.7.b_in, f32[128,128]{1,0:T(8,128)} %get-tuple-element.8.c_in), custom_call_target="tpu_custom_call" | custom-call | tf_op jit(solution)/shard_map/hand_over/pallas_call | solution.py:525

commit v3 on v2

--- a/solution.py
+++ b/solution.py
@@ -75,7 +75,7 @@
     share = tok_send.shape[2]
     tok_count = tokens_ref.shape[0]
     slots = ep * per
-    top = routes_ref.shape[1]
+    top = routes_ref.shape[0]
     owner_count = ep * sp
     z = lax.axis_index("ep")
     x = lax.axis_index("tp")
@@ -124,23 +124,28 @@
     line = lax.broadcasted_iota(jnp.int32, square, 1)
     column = lax.broadcasted_iota(jnp.int32, square, 0)
     lanes = lax.broadcasted_iota(jnp.int32, logits_ref.shape, 1)
-    logits = logits_ref[...]
-    routes = routes_ref[...]
-    picked = jnp.full(logits.shape, -1e30, jnp.float32)
-    named = jnp.zeros(logits.shape, jnp.float32)
-    for j in range(top):
-        route = routes[:, j : j + 1]
-        value = jnp.sum(jnp.where(lanes == route, logits, 0.0), axis=1, keepdims=True)
-        picked = jnp.where(lanes == j, value, picked)
-        named = jnp.where(lanes == top + j, route.astype(jnp.float32), named)
-    raised = jnp.where(
-        lanes < top, jnp.exp(picked - jnp.max(picked, axis=1, keepdims=True)), 0.0
-    )
-    merged = raised / jnp.sum(raised, axis=1, keepdims=True) + named
-    table[me, 0 : 2 * top, :] = merged.T[0 : 2 * top, :]
-    table[me, 2 * top : 3 * top, :] = jnp.broadcast_to(
-        owner_ref[...].astype(jnp.float32), (top, tok_count)
-    )
+    logits_t = logits_ref[...].T
+    routes_t = routes_ref[...]
+    expert_line = lax.broadcasted_iota(jnp.int32, logits_t.shape, 0)
+    picked = jnp.concatenate(
+        [
+            jnp.sum(
+                jnp.where(expert_line == routes_t[i : i + 1, :], logits_t, 0.0),
+                axis=0,
+                keepdims=True,
+            )
+            for i in range(top)
+        ],
+        axis=0,
+    )
+    raised = jnp.exp(picked - jnp.max(picked, axis=0, keepdims=True))
+    table[me, 0:top, :] = raised / jnp.sum(raised, axis=0, keepdims=True)
+    table[me, top : 2 * top, :] = routes_t.astype(jnp.float32)
+    held = jnp.sum(jnp.where(routes_t < ep, routes_t, 0), axis=0, keepdims=True)
+    place = lax.broadcasted_iota(jnp.int32, (top, tok_count), 0)
+    table[me, 2 * top : 3 * top, :] = jnp.where(
+        place == 0, owner_ref[...], jnp.where(place == 1, held, 0)
+    ).astype(jnp.float32)
 
     def table_copy(o):
         return pltpu.make_async_remote_copy(
@@ -165,30 +170,26 @@
     def _(o):
         table_copy(o).wait_recv()
 
-    def gather(o, found):
+    def find(o, found):
         block = table[o]
-        chosen = jnp.where(position == block[2 * top : 2 * top + 1, :], 1.0, 0.0)
-        return found + lax.dot_general(
-            chosen,
-            block,
-            (((1,), (1,)), ((), ())),
-            precision=lax.Precision.HIGHEST,
-            preferred_element_type=jnp.float32,
-        )
-
-    found = lax.fori_loop(
-        0, owner_count, gather, jnp.zeros((tok_count, 3 * top), jnp.float32)
-    )
-    gate_rows = found[:, 0:top]
-    route_rows = jnp.floor(found[:, top : 2 * top] + 0.5)
-    inside = route_rows < ep
-    expert = jnp.sum(jnp.where(inside, route_rows, 0.0), axis=1, keepdims=True)
-    weight = jnp.sum(jnp.where(inside, gate_rows, 0.0), axis=1, keepdims=True)
+        return found + jnp.where(
+            position == block[2 * top : 2 * top + 1, :],
+            block[2 * top + 1 : 2 * top + 2, :],
+            0.0,
+        )
+
+    expert = jnp.sum(
+        lax.fori_loop(0, owner_count, find, jnp.zeros(square, jnp.float32)),
+        axis=1,
+        keepdims=True,
+    )
     expert_square = jnp.broadcast_to(expert, square)
-    same = (expert_square == expert_square.T) & (line < column)
-    rank = jnp.sum(jnp.where(same, 1.0, 0.0), axis=1, keepdims=True)
-    slot = expert * per + rank
-    slot_line = jnp.broadcast_to(slot, square).T[0:1, :]
+    expert_row = expert_square.T[0:1, :]
+    slot_line = expert_row * per + jnp.sum(
+        jnp.where((expert_square == expert_row) & (column < line), 1.0, 0.0),
+        axis=0,
+        keepdims=True,
+    )
     slot_rows = lax.broadcasted_iota(jnp.int32, (slots, tok_count), 0).astype(jnp.float32)
     one_hot = jnp.where(slot_rows == slot_line, 1.0, 0.0)
     pack_ref[...] = one_hot.astype(jnp.bfloat16)
@@ -275,14 +276,40 @@
     def _(k):
         grad_send[k] = slab(grads_ref, pack_grad_ref, peer(k), x)
 
+    z_copy(1, 2).start()
+
     @pl.loop(0, tp)
     def _(h):
         grad_near[h] = slab(grads_ref, pack_grad_ref, peer(1), h)
         grad_all[h, rows_of(z), :] = slab(grads_ref, pack_grad_ref, z, h)
 
+    def gather(o, found):
+        block = table[o]
+        chosen = jnp.where(position == block[2 * top : 2 * top + 1, :], 1.0, 0.0)
+        return found + lax.dot_general(
+            chosen,
+            block,
+            (((1,), (1,)), ((), ())),
+            precision=lax.Precision.HIGHEST,
+            preferred_element_type=jnp.float32,
+        )
+
+    found = lax.fori_loop(
+        0, owner_count, gather, jnp.zeros((tok_count, 3 * top), jnp.float32)
+    )
+    gate_rows = found[:, 0:top]
+    route_rows = found[:, top : 2 * top]
+    inside = route_rows < ep
+    weight = jnp.sum(jnp.where(inside, gate_rows, 0.0), axis=1, keepdims=True)
+    slot = expert * per + jnp.sum(
+        jnp.where((expert_square == expert_row) & (line < column), 1.0, 0.0),
+        axis=1,
+        keepdims=True,
+    )
+    lanes = lax.broadcasted_iota(jnp.int32, logits_ref.shape, 1)
     slot_columns = lax.broadcasted_iota(jnp.int32, (tok_count, slots), 1).astype(jnp.float32)
     unpack_ref[...] = jnp.where(slot_columns == slot, 1.0, 0.0).astype(jnp.bfloat16)
-    coef = jnp.zeros(logits.shape, jnp.float32)
+    coef = jnp.zeros(logits_ref.shape, jnp.float32)
     spread = jnp.where(inside, 1.0, 0.0) - gate_rows
     lane_values = lanes.astype(jnp.float32)
     for j in range(top):
@@ -296,7 +323,10 @@
         z_copy(kind, k).wait_recv()
         x_start(kind, k)
         if kind == 0:
-            z_copy(1, k).start()
+
+            @pl.when(k + 1 < ep)
+            def _():
+                z_copy(1, k + 1).start()
 
     def reduce_rows(kind, k):
         part, recv, back, home = (
@@ -353,12 +383,17 @@
             out_part[h, rows, :] = dot_nn(
                 hid, w_down[:, h * share : (h + 1) * share]
             ).astype(jnp.bfloat16)
-        x_start(2, k)
+
+        @pl.when(k != 1)
+        def _():
+            x_start(2, k)
+
+    x_start(2, jnp.int32(1))
 
     @pl.loop(0, ep)
     def _(k):
         rows = rows_of(peer(k))
-        reduce_rows(2, lax.rem(k + 2, ep))
+        reduce_rows(2, lax.select(k + 2 < ep, k + 2, ep - 1 - k))
 
         @pl.when(k + 2 < ep)
         def _():
@@ -388,13 +423,20 @@
                 dot_nt(grad_gate, w_gate[cols, :]) + dot_nt(grad_up, w_up[cols, :])
             ).astype(jnp.bfloat16)
             tg_part[h, rows, share : share + LANES] = score
-        x_start(3, k)
-
-        @pl.when(k >= 1)
+
+        @pl.when(k >= 2)
+        def _():
+            x_start(3, k)
+
+        @pl.when(k >= 3)
         def _():
             reduce_rows(3, k - 1)
 
+    x_start(3, jnp.int32(1))
+    x_start(3, jnp.int32(0))
     reduce_rows(3, jnp.int32(ep - 1))
+    reduce_rows(3, jnp.int32(1))
+    reduce_rows(3, jnp.int32(0))
 
     @pl.loop(1, ep)
     def _(k):
@@ -431,15 +473,10 @@
                 x_copy(kind, k, j).wait_send()
 
 
-def copy_kernel(a_in, b_in, c_in, a_out, b_out, c_out, sem):
-    copies = [
-        pltpu.make_async_copy(source, target, sem.at[i])
-        for i, (source, target) in enumerate(((a_in, a_out), (b_in, b_out), (c_in, c_out)))
-    ]
-    for copy in copies:
-        copy.start()
-    for copy in copies:
-        copy.wait()
+def copy_kernel(a_in, b_in, c_in, a_out, b_out, c_out):
+    a_out[...] = a_in[...]
+    b_out[...] = b_in[...]
+    c_out[...] = c_in[...]
 
 
 def shards(logits, routes, owner, tokens, out_grad, resp_lengths, w_gate, w_up, w_down):
@@ -513,7 +550,7 @@
         name="expert_layer",
     )(
         logits,
-        routes,
+        routes.T,
         owner.reshape(1, tok_count),
         resp_lengths.reshape(1, 1),
         tokens,
@@ -525,9 +562,8 @@
     return pl.pallas_call(
         copy_kernel,
         out_shape=out_shape,
-        in_specs=[anywhere] * 3,
-        out_specs=(anywhere,) * 3,
-        scratch_shapes=[pltpu.SemaphoreType.DMA((3,))],
+        in_specs=[vmem] * 3,
+        out_specs=(vmem,) * 3,
         name="hand_over",
     )(*results)
 

time: 157 us -> 111 us (0.71)
  Pallas kernels: 153 us -> 109 us
    pallas_call x1, Pallas kernels: 34.9 us -> 2.21 us  [shards(): pl.pallas_call(copy_kernel, out_shape=out_shape, in_specs=[vmem] * 3, out...]
    pallas_call x1, Pallas kernels: 118 us -> 107 us  [shards(): pl.pallas_call(functools.partial(layer_kernel, ep, tp, sp, per), out_shap...]
where the time goes in v3:
time: 111 us; the launch traced here: 110 us
  Pallas kernels  109 us (98%)
  between operations  1.29 us (1%)
    pallas_call x1, Pallas kernels, shards(): pl.pallas_call(functools.partial(layer_kernel, ep, tp, sp, per), out_shap...  107 us

profile of v3, /device:TPU:0, one launch (start us, length us, event | category | flops | bytes accessed | tf_op | source)
XLA Modules:
  0.0 110.4 jit_solution(6309241206750728343)
XLA Ops:
  1.3 106.9 %expert_layer.1 = (bf16[128,2048]{1,0:T(8,128)(2,1)}, bf16[128,2048]{1,0:T(8,128)(2,1)}, f32[128,128]{1,0:T(8,128)}) custom-call(f32[128,128]{1,0:T(8,128)} %logits_ref.1, s32[8,128]{1,0:T(8,128)} %bitcast.4, s32[1,128]{1,0:T(1,128)} %bitcast.5, s32[1,1]{1,0:T(1,128)} %bitcast.3.length_ref, bf16[128,4096]{1,0:T(8,128)(2,1)} %tokens_hbm.1, ...), custom_call_target="tpu_custom_call" | custom-call | flops 9663676416 | bytes 22020096 | tf_op jit(solution)/shard_map/expert_layer/pallas_call | solution.py:502
  108.2 2.2 %hand_over.1 = (bf16[128,2048]{1,0:T(8,128)(2,1)}, bf16[128,2048]{1,0:T(8,128)(2,1)}, f32[128,128]{1,0:T(8,128)}) custom-call(bf16[128,2048]{1,0:T(8,128)(2,1)} %get-tuple-element.6.a_in, bf16[128,2048]{1,0:T(8,128)(2,1)} %get-tuple-element.7.b_in, f32[128,128]{1,0:T(8,128)} %get-tuple-element.8.c_in), custom_call_target="tpu_custom_call" | custom-call | tf_op jit(solution)/shard_map/hand_over/pallas_call | solution.py:562

commit v4 on v3

--- a/solution.py
+++ b/solution.py
@@ -391,13 +391,23 @@
     x_start(2, jnp.int32(1))
 
     @pl.loop(0, ep)
-    def _(k):
+    def _(p):
+        k = lax.select(p == 0, 0, lax.select(p + 1 < ep, p + 1, 1))
         rows = rows_of(peer(k))
-        reduce_rows(2, lax.select(k + 2 < ep, k + 2, ep - 1 - k))
-
-        @pl.when(k + 2 < ep)
-        def _():
-            pump(1, k + 2)
+
+        @pl.when(k >= 3)
+        def _():
+            pump(1, k)
+
+        reduce_rows(2, lax.select(p + 2 < ep, p + 2, ep - 1 - p))
+
+        @pl.when(p == 0)
+        def _():
+            pump(1, 2)
+
+        @pl.when(k >= 3)
+        def _():
+            reduce_rows(3, k - 1)
 
         @pl.when(k == 1)
         def _():
@@ -427,10 +437,6 @@
         @pl.when(k >= 2)
         def _():
             x_start(3, k)
-
-        @pl.when(k >= 3)
-        def _():
-            reduce_rows(3, k - 1)
 
     x_start(3, jnp.int32(1))
     x_start(3, jnp.int32(0))

time: 111 us -> 117 us (1.054)
  Pallas kernels: 109 us -> 115 us
    pallas_call x1, Pallas kernels: 107 us -> 113 us  [shards(): pl.pallas_call(functools.partial(layer_kernel, ep, tp, sp, per), out_shap...]
where the time goes in v4:
time: 117 us
  Pallas kernels  115 us (98%)
  between operations  1.29 us (1%)
    pallas_call x1, Pallas kernels, shards(): pl.pallas_call(functools.partial(layer_kernel, ep, tp, sp, per), out_shap...  113 us

profile of v4, /device:TPU:0, one launch (start us, length us, event | category | flops | bytes accessed | tf_op | source)
XLA Modules:
  0.0 116.7 jit_solution(12221402333864799854)
XLA Ops:
  1.3 113.2 %expert_layer.1 = (bf16[128,2048]{1,0:T(8,128)(2,1)}, bf16[128,2048]{1,0:T(8,128)(2,1)}, f32[128,128]{1,0:T(8,128)}) custom-call(f32[128,128]{1,0:T(8,128)} %logits_ref.1, s32[8,128]{1,0:T(8,128)} %bitcast.4, s32[1,128]{1,0:T(1,128)} %bitcast.5, s32[1,1]{1,0:T(1,128)} %bitcast.3.length_ref, bf16[128,4096]{1,0:T(8,128)(2,1)} %tokens_hbm.1, ...), custom_call_target="tpu_custom_call" | custom-call | flops 9663676416 | bytes 22020096 | tf_op jit(solution)/shard_map/expert_layer/pallas_call | solution.py:508
  114.5 2.2 %hand_over.1 = (bf16[128,2048]{1,0:T(8,128)(2,1)}, bf16[128,2048]{1,0:T(8,128)(2,1)}, f32[128,128]{1,0:T(8,128)}) custom-call(bf16[128,2048]{1,0:T(8,128)(2,1)} %get-tuple-element.6.a_in, bf16[128,2048]{1,0:T(8,128)(2,1)} %get-tuple-element.7.b_in, f32[128,128]{1,0:T(8,128)} %get-tuple-element.8.c_in), custom_call_target="tpu_custom_call" | custom-call | tf_op jit(solution)/shard_map/hand_over/pallas_call | solution.py:568
